TPU v7x, 256 devices: a whole 4x4x8 slice. The times are simulated.
256 devices in a mesh: gy: 4 (over x), gz: 16 (over y, z_lo), ga: 4 (over z_hi, core).
Axes of the slice: x: 4, y: 4, z: 8 (z_hi: 2, z_lo: 4; z = z_hi * 4 + z_lo), core: 2. Of those that a mesh axis runs over, the one named last changes fastest.
Arguments:
- fields: float32 [16, 256, 64, 512], P(None, 'gy', 'gz', 'ga'), may hold values from -6 to 6
- section_start: float32 [16, 256, 64, 512], P(None, 'gy', 'gz', 'ga'), may hold values from -6 to 6
- velocity: float32 [3, 256, 64, 512], P(None, 'gy', 'gz', 'ga'), may hold values from -4 to 4
- diffusivity: float32 [16], replicated, may hold values from 0.02 to 0.2
- reaction: float32 [16, 16], replicated, may hold values from -1.5 to 1.5
- x_factor: bfloat16 [512, 64], replicated, may hold values from -0.25 to 0.25
- y_factor: float32 [256, 64], replicated, may hold values from -6 to 6
Outputs:
- new_fields: float32 [16, 256, 64, 512], P(None, 'gy', 'gz', 'ga')
- x_gram: float32 [512, 512], P(('gy', 'gz'))
- y_products: float32 [64, 256, 64], P(('gz', 'gy'))
All inputs are finite; a program needn't handle non-finite values.
Results may differ from a plain program's by a relative error of at most 0.0028.
Values may be sent and summed in bfloat16 or wider, within the bound.
A program may use at most 64 MiB of HBM per device.

v0:
```python
import jax
import jax.numpy as jnp
from jax import lax
from jax.sharding import PartitionSpec as P

time_step = 0.4


def with_halo(block, sides, width):
    for axis, dim in sides:
        count = lax.axis_size(axis)
        forward = [(i, i + 1) for i in range(count - 1)]
        backward = [(target, source) for source, target in forward]
        low = lax.ppermute(
            lax.slice_in_dim(block, block.shape[dim] - width, None, axis=dim), axis, forward
        )
        high = lax.ppermute(lax.slice_in_dim(block, 0, width, axis=dim), axis, backward)
        block = jnp.concatenate([low, block, high], axis=dim)
    return block


def shards(fields, section_start, velocity, diffusivity, reaction, x_factor, y_factor):
    padded = with_halo(fields, (("gy", 1), ("gz", 2), ("ga", 3)), 1)
    center = padded[:, 1:-1, 1:-1, 1:-1]
    y_plus = padded[:, 2:, 1:-1, 1:-1]
    y_minus = padded[:, :-2, 1:-1, 1:-1]
    z_plus = padded[:, 1:-1, 2:, 1:-1]
    z_minus = padded[:, 1:-1, :-2, 1:-1]
    x_plus = padded[:, 1:-1, 1:-1, 2:]
    x_minus = padded[:, 1:-1, 1:-1, :-2]
    laplace_sum = y_plus + y_minus + z_plus + z_minus + x_plus + x_minus - 6.0 * center
    advection = (
        velocity[0][None] * (x_plus - x_minus) * 0.5
        + velocity[1][None] * (y_plus - y_minus) * 0.5
        + velocity[2][None] * (z_plus - z_minus) * 0.5
    )
    diffusion = diffusivity[:, None, None, None]
    tendency = (
        diffusion * laplace_sum
        - advection
        + jnp.einsum("vw,wyzx->vyzx", reaction, fields, precision=lax.Precision.HIGHEST)
    )
    section_value = 0.75 * section_start + 0.25 * (fields + time_step * tendency)
    buffer_rank = lax.axis_index("ga") == lax.axis_size("ga") - 1
    new_fields = jnp.where(buffer_rank, fields, section_value)
    snapshot = new_fields.astype(jnp.bfloat16)
    devices = lax.axis_size("gy") * lax.axis_size("gz")
    rank_x = x_factor.shape[1]
    gathered = lax.all_gather(snapshot, "ga", axis=3, tiled=True)
    variables, y_cells, z_cells, x_cells = gathered.shape
    unfolded = gathered.reshape(variables * y_cells * z_cells, x_cells)
    cell_count = float(variables * y_cells * z_cells * devices)
    gram_rows = lax.psum_scatter(
        lax.dot_general(
            unfolded, unfolded, (((0,), (0,)), ((), ())), preferred_element_type=jnp.float32
        ),
        ("gy", "gz"),
        scatter_dimension=0,
        tiled=True,
    )
    x_gram = gram_rows / cell_count
    projected = jnp.einsum(
        "vyzx,xr->yzvr", gathered, x_factor, preferred_element_type=jnp.float32
    ).astype(jnp.bfloat16)
    projected = projected.reshape(y_cells, z_cells, variables * rank_x)
    full_y = lax.all_to_all(projected, "gy", split_axis=1, concat_axis=0, tiled=True)
    y_gram = jnp.einsum("yzc,wzc->zyw", full_y, full_y, preferred_element_type=jnp.float32) / float(
        variables * rank_x
    )
    y_products = jnp.einsum("zyw,wk->zyk", y_gram, y_factor, precision=lax.Precision.HIGHEST)
    return (new_fields, x_gram, y_products)


def solution(mesh):
    in_specs = (
        P(None, "gy", "gz", "ga"),
        P(None, "gy", "gz", "ga"),
        P(None, "gy", "gz", "ga"),
        P(),
        P(),
        P(),
        P(),
    )
    out_specs = (P(None, "gy", "gz", "ga"), P(("gy", "gz"), None), P(("gz", "gy"), None, None))
    return jax.shard_map(shards, mesh=mesh, in_specs=in_specs, out_specs=out_specs, check_vma=False)
```

profile of v0, /device:TPU:0, one launch (start us, length us, event | category | flops | bytes accessed | tf_op | source)
XLA Modules:
  0.0 534.6 jit_solution(17239178171794730020)
XLA Ops:
  7.2 0.0 copy-start
  7.2 0.0 copy-start.1
  7.2 0.0 all-gather.2.cloned.1.call-start
  7.2 3.0 copy.52
  10.2 0.0 copy-start.4
  10.2 1.7 collective-permute-start.1
  11.9 1.3 collective-permute-start
  13.2 0.3 collective-permute-done.1
  13.5 0.0 copy-start.11
  13.5 0.0 copy-done.1
  13.5 1.2 constant_dynamic-update-slice_fusion.1
  14.7 0.0 copy-done.4
  14.7 0.0 copy-done.11
  14.7 3.0 collective-permute-done
  17.7 0.0 copy-start.13
  17.7 0.0 copy-start.2
  17.7 0.1 fusion.13
  17.8 1.3 collective-permute-start.2
  19.1 4.6 collective-permute-start.3
  23.7 8.8 %collective-permute-done.2 = f32[16,66,1,128]{3,0,2,1:T(8,128)S(1)} collective-permute-done((f32[16,66,1,128]{3,0,2,1:T(8,128)S(1)}, f32[16,66,1,128]{3,0,2,1:T(8,128)S(1)}, u32[]{:S(2)}, u32[]{:S(2)}) %collective-permute-start.2) | collective-permute-done | bytes 540704 | tf_op jit(solution)/shard_map/ppermute | solution.py:17
  32.5 0.0 copy-done.13
  32.5 1.2 collective-permute-done.3
  33.6 0.0 copy-done.2
  33.6 0.0 copy-done.6
  33.6 0.8 copy-done.8
  34.4 0.3 pad_maximum_fusion
  34.8 2.9 fusion.12
  37.6 2.8 copy.45
  40.4 1.3 collective-permute-start.4
  41.7 2.2 copy.47
  43.9 3.6 collective-permute-start.5
  47.5 1.7 slice_bitcast_fusion.2
  49.3 0.0 collective-permute-done.4
  49.3 2.6 copy.46
  51.9 0.0 copy-start.14
  51.9 0.0 copy-start.15
  51.9 0.0 collective-permute-done.5
  52.0 3.6 copy.48
  55.5 0.0 copy-done.3
  55.5 0.0 copy-done.7
  55.5 0.0 copy-done.9
  55.5 0.0 copy-done.12
  55.6 0.0 copy-done.14
  55.6 0.0 copy-done.15
  55.6 10.5 %fusion.15 = (bf16[16,64,4,128]{3,0,2,1:T(8,128)(2,1)}, f32[16,64,4,128]{3,0,2,1:T(8,128)}) fusion(f32[16,64,4,128]{3,0,2,1:T(8,128)} %copy-done.4, f32[16,16]{1,0:T(8,128)S(1)} %copy-done.14, f32[64,4,128]{2,1,0:T(4,128)} %get-tuple-element.19, f32[64,4,128]{2,1,0:T(4,128)} %get-tuple-element.20, f32[64,4,128]{2,1,0:T(4,128)S(1)} %get-tuple-element.18, ...), kind=kOutput, calls=%fused_computation.33 | convolution fusion | flops 119537664 | bytes 11094593 | tf_op jit(solution)/shard_map/vw,wyzx->vyzx/dot_general | solution.py:41
  66.0 0.0 all-gather.2.cloned.1.call-update
  66.1 0.2 reduce-scatter.2.cloned.1.call-start
  66.3 83.5 %all-gather.2.cloned.1.call-done = bf16[16,64,4,512]{3,0,2,1:T(8,128)(2,1)} async-done(((bf16[16,64,4,128]{3,0,2,1:T(8,128)(2,1)}), bf16[16,64,4,512]{3,0,2,1:T(8,128)(2,1)}) %all-gather.2.cloned.1.call-update) | async-done | bytes 4194320 | tf_op jit(solution)/shard_map/all_gather | solution.py:49
  149.8 6.8 %convolution_bitcast_fusion = f32[512,512]{1,0:T(8,128)} fusion(bf16[16,64,4,512]{3,0,2,1:T(8,128)(2,1)} %all-gather.2.cloned.1.call-done), kind=kOutput, calls=%fused_computation.18 | convolution fusion | flops 2147483648 | bytes 5242880 | tf_op jit(solution)/shard_map/dot_general | solution.py:54
  156.6 0.0 reduce-scatter.2.cloned.1.call-update
  156.6 0.0 copy-done
  156.6 6.9 %fusion.7 = bf16[64,4,16,64]{3,0,1,2:T(8,128)(2,1)S(1)} fusion(bf16[16,64,4,512]{3,0,2,1:T(8,128)(2,1)} %all-gather.2.cloned.1.call-done, bf16[512,64]{0,1:T(8,128)(2,1)S(1)} %copy-done), kind=kOutput, calls=%fused_computation.17 | convolution fusion | flops 268697600 | bytes 4784128 | tf_op jit(solution)/shard_map/vyzx,xr->yzvr/dot_general | solution.py:62
  163.5 0.0 copy-start.5
  163.5 0.7 copy.54
  164.2 1.5 reshape.22
  165.8 4.2 all-to-all-start
  170.0 0.0 copy-done.5
  170.0 2.1 copy.55
  172.1 7.8 %all-to-all-done = bf16[64,4,1024]{2,0,1:T(8,128)(2,1)S(1)} async-done(((bf16[64,4,1024]{2,0,1:T(8,128)(2,1)}), bf16[64,4,1024]{2,0,1:T(8,128)(2,1)S(1)}, u32[]{:S(2)}, u32[]{:S(2)}) %all-to-all-start) | async-done | bytes 524320 | tf_op jit(solution)/shard_map/all_to_all | solution.py:66
  179.9 0.3 convolution_multiply_fusion
  180.3 0.0 copy-done.10
  180.3 1.0 convolution_bitcast_fusion.1
  181.3 345.1 %reduce-scatter.2.cloned.1.call-done = f32[8,512]{1,0:T(8,128)} async-done(((f32[512,512]{1,0:T(8,128)}), f32[8,512]{1,0:T(8,128)}) %reduce-scatter.2.cloned.1.call-update) | async-done | bytes 16400 | tf_op jit(solution)/shard_map/reduce_scatter | solution.py:53
  526.4 1.3 broadcast_multiply_fusion
  (10 shorter events, 0.0 us)
Async XLA Ops:
  7.2 149.4 %copy-start = (bf16[512,64]{0,1:T(8,128)(2,1)S(1)}, bf16[512,64]{0,1:T(8,128)(2,1)}, u32[]{:S(2)}) copy-start(bf16[512,64]{0,1:T(8,128)(2,1)} %param.12) | copy-start | bytes 196612
  7.2 6.3 %copy-start.1 = (f32[16,64,4,128]{3,2,1,0:T(4,128)S(1)}, f32[16,64,4,128]{3,2,1,0:T(4,128)}, u32[]{:S(2)}) copy-start(f32[16,64,4,128]{3,2,1,0:T(4,128)} %param.7) | copy-start | bytes 6291460
  7.2 142.6 %all-gather.2.cloned.1.call-start = ((), (), s32[]{:S(2)}) async-start(), calls=%async_computation.2 | async-start | bytes 5242880 | tf_op jit(solution)/shard_map/all_gather | solution.py:49
  10.2 4.5 copy-start.4
  10.2 3.2 collective-permute-start.1
  11.9 5.8 %collective-permute-start = (f32[16,1,4,128]{3,0,2,1:T(8,128)S(1)}, f32[16,1,4,128]{3,0,2,1:T(8,128)S(1)}, u32[]{:S(2)}, u32[]{:S(2)}) collective-permute-start(f32[16,1,4,128]{3,0,2,1:T(8,128)S(1)} %get-tuple-element.16), channel_id=1, source_target_pairs={{64,0},{128,64},{192,128},{65,1},{129,65},{193,129},{66,2},{130,66... | collective-permute-start | bytes 98312 | tf_op jit(solution)/shard_map/ppermute | solution.py:17
  13.5 1.2 copy-start.11
  17.7 14.8 %copy-start.13 = (f32[16,1,4,128]{3,0,2,1:T(8,128)}, f32[16,1,4,128]{3,0,2,1:T(8,128)S(1)}, u32[]{:S(2)}) copy-start(f32[16,1,4,128]{3,0,2,1:T(8,128)S(1)} %collective-permute-done) | copy-start | bytes 98308
  17.7 15.9 %copy-start.2 = (f32[16,66,4,128]{3,0,2,1:T(8,128)}, f32[16,66,4,128]{3,0,2,1:T(8,128)S(1)}, u32[]{:S(2)}) copy-start(f32[16,66,4,128]{3,0,2,1:T(8,128)S(1)} %constant_dynamic-update-slice_fusion) | copy-start | bytes 6488068
  17.8 14.7 %collective-permute-start.2 = (f32[16,66,1,128]{3,0,2,1:T(8,128)S(1)}, f32[16,66,1,128]{3,0,2,1:T(8,128)S(1)}, u32[]{:S(2)}, u32[]{:S(2)}) collective-permute-start(f32[16,66,1,128]{3,0,2,1:T(8,128)S(1)} %get-tuple-element.15), channel_id=1, source_target_pairs={{4,0},{8,4},{12,8},{16,12},{20,16},{24,20},{28,24},{32,28},{36,32}... | collective-permute-start | bytes 1622024 | tf_op jit(solution)/shard_map/ppermute | solution.py:17
  19.1 14.5 %collective-permute-start.3 = (f32[16,66,1,128]{3,0,2,1:T(8,128)S(1)}, f32[16,66,1,128]{3,0,2,1:T(8,128)S(1)}, u32[]{:S(2)}, u32[]{:S(2)}) collective-permute-start(f32[16,66,1,128]{3,0,2,1:T(8,128)S(1)} %get-tuple-element.14), channel_id=1, source_target_pairs={{0,4},{4,8},{8,12},{12,16},{16,20},{20,24},{24,28},{28,32},{32,36}... | collective-permute-start | bytes 1622024 | tf_op jit(solution)/shard_map/ppermute | solution.py:14
  32.5 1.2 copy-start.6
  33.6 0.8 copy-start.8
  40.4 8.9 %collective-permute-start.4 = (f32[16,66,6,1]{1,0,3,2:T(8,128)S(1)}, f32[16,66,6,1]{1,0,3,2:T(8,128)S(1)}, u32[]{:S(2)}, u32[]{:S(2)}) collective-permute-start(f32[16,66,6,1]{1,0,3,2:T(8,128)S(1)} %copy.45), channel_id=1, source_target_pairs={{1,0},{2,1},{3,2},{5,4},{6,5},{7,6},{9,8},{10,9},{11,10},{13,12},{... | collective-permute-start | bytes 76040 | tf_op jit(solution)/shard_map/ppermute | solution.py:17
  43.9 8.0 %collective-permute-start.5 = (f32[16,66,6,1]{1,0,3,2:T(8,128)}, f32[16,66,6,1]{1,0,3,2:T(8,128)}, u32[]{:S(2)}, u32[]{:S(2)}) collective-permute-start(f32[16,66,6,1]{1,0,3,2:T(8,128)} %copy.47), channel_id=1, source_target_pairs={{0,1},{1,2},{2,3},{4,5},{5,6},{6,7},{8,9},{9,10},{10,11},{12,13},{... | collective-permute-start | bytes 76040 | tf_op jit(solution)/shard_map/ppermute | solution.py:14
  51.9 3.6 copy-start.3
  51.9 3.6 copy-start.7
  51.9 3.6 copy-start.9
  51.9 3.6 copy-start.12
  51.9 3.6 copy-start.14
  51.9 3.6 copy-start.15
  66.1 460.4 %reduce-scatter.2.cloned.1.call-start = ((), (), s32[]{:S(2)}) async-start(), calls=%async_computation.3 | async-start | bytes 1064960 | tf_op jit(solution)/shard_map/reduce_scatter | solution.py:53
  163.5 6.5 %copy-start.5 = (f32[16,64,4,128]{3,0,2,1:T(8,128)S(1)}, f32[16,64,4,128]{3,0,2,1:T(8,128)}, u32[]{:S(2)}) copy-start(f32[16,64,4,128]{3,0,2,1:T(8,128)} %get-tuple-element.22) | copy-start | bytes 6291460
  165.8 14.2 %all-to-all-start = ((bf16[64,4,1024]{2,0,1:T(8,128)(2,1)}), bf16[64,4,1024]{2,0,1:T(8,128)(2,1)S(1)}, u32[]{:S(2)}, u32[]{:S(2)}) async-start(bf16[64,4,1024]{2,0,1:T(8,128)(2,1)} %reshape.22), calls=%async_computation.1 | async-start | bytes 1048576 | tf_op jit(solution)/shard_map/all_to_all | solution.py:66
  170.0 10.2 %copy-start.10 = (f32[256,64]{0,1:T(8,128)S(1)}, f32[256,64]{0,1:T(8,128)}, u32[]{:S(2)}) copy-start(f32[256,64]{0,1:T(8,128)} %param.13) | copy-start | bytes 196612
Sparse Core Ops, SparseCore 0:
  66.2 83.5 all-gather.1
  156.7 369.6 reduce-scatter.1
where the time goes:
time: 535 us
  waiting for transfers between devices  450 us (84%)
  matrix products  25.5 us (5%)
  local copies, waits for them, and re-layouts  25.3 us (5%)
  starting transfers between devices  18.3 us (3%)
  between operations  14.3 us (3%)
    reduce_scatter x1, waiting for transfers between devices, shards(): lax.psum_scatter(lax.dot_general(unfolded, unfolded, (((0,), (0,)), ((),...  345 us
    all_gather x1, waiting for transfers between devices, shards(): gathered = lax.all_gather(snapshot, 'ga', axis=3, tiled=True)  83.5 us
    ppermute x3, waiting for transfers between devices, with_halo(): lax.ppermute(lax.slice_in_dim(block, 0, width, axis=dim), axis, backward)  11.8 us
  transfers between devices with their start and end apart: 9, of which 7 were waited for; matrix products, arithmetic and copies ran while one was open for 4% of the time, Pallas kernels for 0%

commit v1 on v0

v1 whole, which is shorter than its diff:
```python
import functools

import jax
import jax.numpy as jnp
from jax import lax
from jax.experimental import pallas as pl
from jax.experimental.pallas import tpu as pltpu
from jax.sharding import PartitionSpec as P

time_step = 0.4

MESH = pl.DeviceIdType.MESH
V = 16
YN = 64
ZN = 4
XN = 128
ROWS = YN * ZN
NC = 4
YC = YN // NC
CR = YC * ZN
PAD = 8
NY, NZ, NA = 4, 16, 4
F32, BF16 = jnp.float32, jnp.bfloat16


def bring(src, dst, send_sem, recv_sem, device):
    return pltpu.make_async_remote_copy(
        src_ref=src, dst_ref=dst, send_sem=send_sem, recv_sem=recv_sem, device_id=device, device_id_type=MESH
    )


def kernel(
    dif, rea, xft, yft, fields, start, vel,
    new_out, gram_out, yprod_out,
    fbuf, sbuf, vbuf, obuf, zsend, zrecv, xpack, xrecv, xcomb, snap, full, kmat, rfb,
    gacc, r1, g2, r2, s2, r3, pbuf, mbuf, ysend, yrecv,
    load_sem, out_sem, zs_sem, zr_sem, ys_sem, yr_sem, xs_sem, xr_sem, as_sem, ar_sem,
    ps_sem, pr_sem, bs_sem, br_sem, s1_sem, r1_sem, s2_sem, r2_sem, s3_sem, r3_sem,
):
    gy, gz, ga = lax.axis_index("gy"), lax.axis_index("gz"), lax.axis_index("ga")
    cy, cz = gz // 4, gz % 4
    zhi, core = ga // 2, ga % 2
    plane = gy * 4 + cy
    column = (zhi * 4 + cz) * 2 + core
    buffer_slab = ga == NA - 1
    inner_slab = ga < NA - 1

    def plane_device(index):
        return (index // 4, (index % 4) * 4 + cz, ga)

    def column_device(index):
        return (gy, cy * 4 + (index // 2) % 4, (index // 8) * 2 + index % 2)

    load_f = pltpu.make_async_copy(fields, fbuf.at[:, pl.ds(PAD, ROWS), :], load_sem.at[0])
    load_s = pltpu.make_async_copy(start, sbuf, load_sem.at[1])
    load_v = pltpu.make_async_copy(vel, vbuf, load_sem.at[2])
    load_f.start()
    load_s.start()
    load_v.start()

    barrier = pltpu.get_barrier_semaphore()
    wrap_up = jnp.logical_and(cz == 3, gz < NZ - 1)
    wrap_down = jnp.logical_and(cz == 0, gz > 0)

    @pl.when(wrap_up)
    def _():
        pl.semaphore_signal(barrier, inc=1, device_id=(gy, gz + 1, ga), device_id_type=MESH)

    @pl.when(wrap_down)
    def _():
        pl.semaphore_signal(barrier, inc=1, device_id=(gy, gz - 1, ga), device_id_type=MESH)

    def greet(j, carry):
        pl.semaphore_signal(barrier, inc=1, device_id=plane_device((plane + j) % 16), device_id_type=MESH)
        pl.semaphore_signal(barrier, inc=1, device_id=column_device((column + j) % 16), device_id_type=MESH)
        return carry

    lax.fori_loop(1, 16, greet, 0)

    @pl.when(gy == 0)
    def _():
        fbuf[:, 0:PAD, :] = jnp.zeros((V, PAD, XN), F32)

    @pl.when(gy == NY - 1)
    def _():
        fbuf[:, PAD + ROWS : PAD + ROWS + PAD, :] = jnp.zeros((V, PAD, XN), F32)

    @pl.when(gz == 0)
    def _():
        zrecv[0] = jnp.zeros((NC, V, YC, XN), BF16)

    @pl.when(gz == NZ - 1)
    def _():
        zrecv[1] = jnp.zeros((NC, V, YC, XN), BF16)

    @pl.when(ga == 0)
    def _():
        xrecv[0] = jnp.zeros((YN, XN), F32)

    low16 = lax.broadcasted_iota(jnp.int32, (V * YC, V), 0) // YC
    spread = (low16 == lax.broadcasted_iota(jnp.int32, (V * YC, V), 1)).astype(F32).astype(BF16)
    rows_at = lax.broadcasted_iota(jnp.int32, (V * YC, V * YC), 0) % YC
    cols_at = lax.broadcasted_iota(jnp.int32, (V * YC, V * YC), 1) % YC
    same = rows_at == cols_at
    rate = (0.25 * time_step) * rea[...]
    rate_high = rate.astype(BF16)
    rate_low = (rate - rate_high.astype(F32)).astype(BF16)
    for part, piece in enumerate((rate_high, rate_low)):
        tall = jnp.dot(spread, piece, preferred_element_type=F32).astype(BF16)
        square = lax.dot_general(tall, spread, (((1,), (1,)), ((), ())), preferred_element_type=F32)
        kmat[part] = jnp.where(same, square, 0.0).astype(BF16)

    load_f.wait()

    @pl.when(inner_slab)
    def _():
        def face(v, carry):
            for side, z in ((0, 0), (1, ZN - 1)):
                for c in range(NC):
                    piece = fbuf[v, pl.ds(PAD + c * CR + z, YC, stride=ZN), :]
                    zsend[side, c, v] = piece.astype(BF16)
            return carry

        lax.fori_loop(0, V, face, 0)

    pl.semaphore_wait(barrier, 30 + wrap_up.astype(jnp.int32) + wrap_down.astype(jnp.int32))

    def z_copy(side, c):
        return bring(
            zsend.at[side, c], zrecv.at[1 - side, c], zs_sem.at[side, c], zr_sem.at[1 - side, c],
            (gy, gz - 1 + 2 * side, ga),
        )

    low_z = jnp.logical_and(inner_slab, gz > 0)
    high_z = jnp.logical_and(inner_slab, gz < NZ - 1)
    low_y = jnp.logical_and(inner_slab, gy > 0)
    high_y = jnp.logical_and(inner_slab, gy < NY - 1)

    def y_copy(side):
        src = fields.at[:, pl.ds((ROWS - PAD) * side, PAD), :]
        dst = fbuf.at[:, pl.ds((PAD + ROWS) * (1 - side), PAD), :]
        return bring(src, dst, ys_sem.at[side], yr_sem.at[1 - side], (gy - 1 + 2 * side, gz, ga))

    for c in range(NC):
        @pl.when(low_z)
        def _():
            z_copy(0, c).start()

        @pl.when(high_z)
        def _():
            z_copy(1, c).start()

        if c == 0:
            @pl.when(low_y)
            def _():
                y_copy(0).start()

            @pl.when(high_y)
            def _():
                y_copy(1).start()

    lane = lax.broadcasted_iota(jnp.int32, (YN, XN), 1)

    def pack(v, acc):
        for z in range(ZN):
            at = 2 * (v * ZN + z)
            piece = fbuf[v, pl.ds(PAD + z, YN, stride=ZN), :]
            moved = pltpu.roll(piece, at + 1, 1)
            acc = jnp.where(jnp.logical_or(lane == at, lane == at + 1), moved, acc)
        return acc

    xpack[...] = lax.fori_loop(0, V, pack, jnp.zeros((YN, XN), F32))

    def x_copy(side):
        return bring(
            xpack, xrecv.at[1 - side], xs_sem.at[side], xr_sem.at[1 - side], (gy, gz, ga - 1 + 2 * side)
        )

    low_x = ga > 0
    high_x = ga < NA - 2

    @pl.when(low_x)
    def _():
        x_copy(0).start()

    @pl.when(high_x)
    def _():
        x_copy(1).start()

    def exchange(c, j):
        peer = (ga + j) % NA
        return bring(snap.at[c, peer], full.at[c, ga], as_sem.at[c, j], ar_sem.at[c, ga], (gy, gz, peer))

    def arrived(c, j):
        slab = (ga + j) % NA
        return bring(snap.at[c, slab], full.at[c, slab], as_sem.at[c, j], ar_sem.at[c, slab], (gy, gz, slab))

    def store_out(c):
        rows = pl.ds(c * CR, CR)
        return pltpu.make_async_copy(obuf.at[:, rows, :], new_out.at[:, rows, :], out_sem.at[c])

    def hand_over(c):
        full[c, ga] = snap[c, ga]
        for j in (2, 3, 1):
            exchange(c, j).start()
        store_out(c).start()

    load_s.wait()
    load_v.wait()

    @pl.when(buffer_slab)
    def _():
        def chunk(c, carry):
            def variable(v, inner):
                obuf[v, pl.ds(c * CR, CR), :] = fbuf[v, pl.ds(PAD + c * CR, CR), :]
                for z in range(ZN):
                    piece = fbuf[v, pl.ds(PAD + c * CR + z, YC, stride=ZN), :]
                    snap[c, z, v] = piece.astype(BF16)
                return inner

            lax.fori_loop(0, V, variable, 0)
            hand_over(c)
            return carry

        lax.fori_loop(0, NC, chunk, 0)

    @pl.when(inner_slab)
    def _():
        @pl.when(gy > 0)
        def _():
            y_copy(1).wait_recv()

        @pl.when(gy < NY - 1)
        def _():
            y_copy(0).wait_recv()

        @pl.when(ga > 0)
        def _():
            x_copy(1).wait_recv()

        x_copy(0).wait_recv()
        xcomb[...] = jnp.where(lane % 2 == 0, xrecv[0], xrecv[1])
        edge = lax.broadcasted_iota(jnp.int32, (YC, XN), 1)

        def chunk(c, carry):
            @pl.when(gz > 0)
            def _():
                z_copy(1, c).wait_recv()

            @pl.when(gz < NZ - 1)
            def _():
                z_copy(0, c).wait_recv()

            for z in range(ZN):
                first = PAD + c * CR + z
                stack = jnp.concatenate(
                    [fbuf[v, pl.ds(first, YC, stride=ZN), :] for v in range(V)], axis=0
                )
                high = stack.astype(BF16)
                low = (stack - high.astype(F32)).astype(BF16)
                reacted = (
                    jnp.dot(kmat[0], high, preferred_element_type=F32)
                    + jnp.dot(kmat[0], low, preferred_element_type=F32)
                    + jnp.dot(kmat[1], high, preferred_element_type=F32)
                )
                rfb[...] = reacted.reshape(V, YC, XN)
                scale = 0.125 * time_step
                vx, vy, vz = (scale * vbuf[d, pl.ds(c * CR + z, YC, stride=ZN), :] for d in range(3))
                faces = xcomb[pl.ds(c * YC, YC), :]

                def variable(v, inner):
                    here = fbuf[v, pl.ds(first, YC, stride=ZN), :]
                    y_plus = fbuf[v, pl.ds(first + ZN, YC, stride=ZN), :]
                    y_minus = fbuf[v, pl.ds(first - ZN, YC, stride=ZN), :]
                    if z < ZN - 1:
                        z_plus = fbuf[v, pl.ds(first + 1, YC, stride=ZN), :]
                    else:
                        z_plus = zrecv[1, c, v].astype(F32)
                    if z > 0:
                        z_minus = fbuf[v, pl.ds(first - 1, YC, stride=ZN), :]
                    else:
                        z_minus = zrecv[0, c, v].astype(F32)
                    at = 2 * (v * ZN + z)
                    moved = pltpu.roll(faces, XN - 1 - at, 1)
                    x_plus = pltpu.roll(jnp.where(edge == 0, moved, here), XN - 1, 1)
                    x_minus = pltpu.roll(jnp.where(edge == XN - 1, moved, here), 1, 1)
                    laplace = (
                        (x_plus + x_minus) + (y_plus + y_minus) + (z_plus + z_minus) - 6.0 * here
                    )
                    advection = (
                        vx * (x_plus - x_minus) + vy * (y_plus - y_minus) + vz * (z_plus - z_minus)
                    )
                    began = sbuf[v, pl.ds(c * CR + z, YC, stride=ZN), :]
                    value = (
                        0.75 * began + 0.25 * here
                        + ((0.25 * time_step) * dif[v]) * laplace - advection + rfb[v]
                    )
                    obuf[v, pl.ds(c * CR + z, YC, stride=ZN), :] = value
                    snap[c, z, v] = value.astype(BF16)
                    return inner

                lax.fori_loop(0, V, variable, 0, unroll=True)
            hand_over(c)
            return carry

        lax.fori_loop(0, NC, chunk, 0)

    diagonal = gy == ga
    diagonal_device = (ga, gz, ga)

    def project_copy(c):
        return bring(
            pbuf.at[c], mbuf.at[:, gy * NC + c], ps_sem.at[c], pr_sem.at[gy * NC + c], diagonal_device
        )

    zero = jnp.zeros_like(xft[...])
    first_half = jnp.concatenate([xft[...], zero], axis=0)
    second_half = jnp.concatenate([zero, xft[...]], axis=0)
    nt = (((1,), (1,)), ((), ()))
    tn = (((0,), (0,)), ((), ()))

    def gather_gram(c, carry):
        for j in range(1, NA):
            arrived(c, j).wait_recv()
        wide = jnp.concatenate([full[c, s].reshape(V * YC, XN) for s in range(NA)], axis=1)
        for i in range(2):
            half = (core + 1 + i) % 2
            part = jnp.concatenate(
                [full[c, 2 * half + s].reshape(V * YC, XN) for s in range(2)], axis=1
            )
            term = lax.dot_general(wide, part, tn, preferred_element_type=F32)

            @pl.when(c == 0)
            def _():
                gacc[i] = term

            @pl.when(c > 0)
            def _():
                gacc[i] = gacc[i] + term

            if i == 0:
                @pl.when(c == NC - 1)
                def _():
                    bring(gacc.at[0], r1, s1_sem, r1_sem, (gy, gz, zhi * 2 + 1 - core)).start()

        rows = V * YC // 2
        projected = lax.dot_general(wide[:rows], first_half, nt, preferred_element_type=F32)
        projected += lax.dot_general(wide[rows:], second_half, nt, preferred_element_type=F32)
        projected = projected.astype(BF16).reshape(V // 2, YC, XN)

        @pl.when(diagonal)
        def _():
            mbuf[:, gy * NC + c] = projected

        @pl.when(jnp.logical_not(diagonal))
        def _():
            pbuf[c] = projected
            project_copy(c).start()

        return carry

    lax.fori_loop(0, NC, gather_gram, 0)

    pair = bring(gacc.at[0], r1, s1_sem, r1_sem, (gy, gz, zhi * 2 + 1 - core))
    pair.wait_recv()
    g2[...] = (gacc[1] + r1[...]).astype(BF16).reshape(16, 32, 256)

    def plane_copy(j):
        to = (plane + j) % 16
        return bring(g2.at[to], r2.at[plane], s2_sem.at[j], r2_sem.at[plane], plane_device(to))

    def plane_arrived(j):
        source = (plane + j) % 16
        return bring(g2.at[source], r2.at[source], s2_sem.at[j], r2_sem.at[source], plane_device(source))

    def start_plane(j, carry):
        plane_copy(j).start()
        return carry

    lax.fori_loop(1, 16, start_plane, 0)

    def bcast_copy(j):
        peer = (ga + j) % NA
        return bring(ysend, yrecv, bs_sem.at[j], br_sem, (gy, gz, peer))

    @pl.when(diagonal)
    def _():
        def wait_projected(i, carry):
            slot = (gy * NC + NC + i) % 16
            bring(
                pbuf.at[0], mbuf.at[:, slot], ps_sem.at[0], pr_sem.at[slot], diagonal_device
            ).wait_recv()
            return carry

        lax.fori_loop(0, 3 * NC, wait_projected, 0)
        y_gram = jnp.zeros((256, 256), F32)
        for i in range(V // 2):
            layer = mbuf[i].reshape(256, XN)
            y_gram += lax.dot_general(layer, layer, nt, preferred_element_type=F32)
        product = jnp.dot(
            yft[...], y_gram * (1.0 / 1024.0), precision=lax.Precision.HIGHEST, preferred_element_type=F32
        )
        ysend[...] = product
        yprod_out[...] = product
        for j in (2, 3, 1):
            bcast_copy(j).start()

    def add_plane(j, acc):
        plane_arrived(j).wait_recv()
        return acc + r2[(plane + j) % 16].astype(F32)

    total = lax.fori_loop(1, 16, add_plane, g2[plane].astype(F32))
    s2[...] = total.reshape(4, 8, 256)
    r3[column] = s2[cz]

    def column_copy(j):
        to = (column + j) % 16
        return bring(s2.at[(to // 2) % 4], r3.at[column], s3_sem.at[j], r3_sem.at[column], column_device(to))

    def column_arrived(j):
        source = (column + j) % 16
        return bring(s2.at[0], r3.at[source], s3_sem.at[j], r3_sem.at[source], column_device(source))

    def start_column(j, carry):
        column_copy(j).start()
        return carry

    lax.fori_loop(1, 16, start_column, 0)

    @pl.when(low_z)
    def _():
        for c in range(NC):
            z_copy(0, c).wait_send()

    @pl.when(high_z)
    def _():
        for c in range(NC):
            z_copy(1, c).wait_send()

    @pl.when(low_y)
    def _():
        y_copy(0).wait_send()

    @pl.when(high_y)
    def _():
        y_copy(1).wait_send()

    @pl.when(low_x)
    def _():
        x_copy(0).wait_send()

    @pl.when(high_x)
    def _():
        x_copy(1).wait_send()

    def sent(c, carry):
        for j in range(1, NA):
            exchange(c, j).wait_send()
        store_out(c).wait()

        @pl.when(jnp.logical_not(diagonal))
        def _():
            project_copy(c).wait_send()

        return carry

    lax.fori_loop(0, NC, sent, 0)
    pair.wait_send()

    def plane_sent(j, carry):
        plane_copy(j).wait_send()
        return carry

    lax.fori_loop(1, 16, plane_sent, 0)

    @pl.when(diagonal)
    def _():
        for j in range(1, NA):
            bcast_copy(j).wait_send()

    @pl.when(jnp.logical_not(diagonal))
    def _():
        bcast_copy(1).wait_recv()
        yprod_out[...] = yrecv[...]

    def column_wait(j, carry):
        column_arrived(j).wait_recv()
        return carry

    lax.fori_loop(1, 16, column_wait, 0)
    cells = 1.0 / float(V * 256 * 64)
    for half in range(2):
        acc = r3[half]
        for z in range(1, 8):
            acc = acc + r3[2 * z + half]
        gram_out[:, 256 * half : 256 * (half + 1)] = acc * cells

    def column_sent(j, carry):
        column_copy(j).wait_send()
        return carry

    lax.fori_loop(1, 16, column_sent, 0)


def shards(fields, section_start, velocity, diffusivity, reaction, x_factor, y_factor):
    vmem = pl.BlockSpec(memory_space=pltpu.VMEM)
    hbm = pl.BlockSpec(memory_space=pl.ANY)
    dma = pltpu.SemaphoreType.DMA
    new_fields, gram, product = pl.pallas_call(
        kernel,
        out_shape=(
            jax.ShapeDtypeStruct((V, ROWS, XN), F32),
            jax.ShapeDtypeStruct((8, 512), F32),
            jax.ShapeDtypeStruct((64, 256), F32),
        ),
        in_specs=[pl.BlockSpec(memory_space=pltpu.SMEM), vmem, vmem, vmem, hbm, hbm, hbm],
        out_specs=(hbm, vmem, vmem),
        scratch_shapes=[
            pltpu.VMEM((V, PAD + ROWS + PAD, XN), F32),
            pltpu.VMEM((V, ROWS, XN), F32),
            pltpu.VMEM((3, ROWS, XN), F32),
            pltpu.VMEM((V, ROWS, XN), F32),
            pltpu.VMEM((2, NC, V, YC, XN), BF16),
            pltpu.VMEM((2, NC, V, YC, XN), BF16),
            pltpu.VMEM((YN, XN), F32),
            pltpu.VMEM((2, YN, XN), F32),
            pltpu.VMEM((YN, XN), F32),
            pltpu.VMEM((NC, ZN, V, YC, XN), BF16),
            pltpu.VMEM((NC, NA, V, YC, XN), BF16),
            pltpu.VMEM((2, V * YC, V * YC), BF16),
            pltpu.VMEM((V, YC, XN), F32),
            pltpu.VMEM((2, 512, 256), F32),
            pltpu.VMEM((512, 256), F32),
            pltpu.VMEM((16, 32, 256), BF16),
            pltpu.VMEM((16, 32, 256), BF16),
            pltpu.VMEM((4, 8, 256), F32),
            pltpu.VMEM((16, 8, 256), F32),
            pltpu.VMEM((NC, V // 2, YC, XN), BF16),
            pltpu.VMEM((V // 2, 16, YC, XN), BF16),
            pltpu.VMEM((64, 256), F32),
            pltpu.VMEM((64, 256), F32),
            dma((3,)), dma((NC,)),
            dma((2, NC)), dma((2, NC)), dma((2,)), dma((2,)), dma((2,)), dma((2,)),
            dma((NC, NA)), dma((NC, NA)),
            dma((NC,)), dma((16,)), dma((NA,)), dma,
            dma, dma, dma((16,)), dma((16,)), dma((16,)), dma((16,)),
        ],
        compiler_params=pltpu.CompilerParams(
            collective_id=0, has_side_effects=True, vmem_limit_bytes=40 << 20
        ),
        name="section",
    )(
        diffusivity,
        reaction,
        x_factor.T,
        y_factor.T,
        fields.reshape(V, ROWS, XN),
        section_start.reshape(V, ROWS, XN),
        velocity.reshape(3, ROWS, XN),
    )
    return new_fields.reshape(V, YN, ZN, XN), gram, product.T[None]


def solution(mesh):
    in_specs = (
        P(None, "gy", "gz", "ga"),
        P(None, "gy", "gz", "ga"),
        P(None, "gy", "gz", "ga"),
        P(),
        P(),
        P(),
        P(),
    )
    out_specs = (P(None, "gy", "gz", "ga"), P(("gy", "gz"), None), P(("gz", "gy"), None, None))
    return jax.shard_map(shards, mesh=mesh, in_specs=in_specs, out_specs=out_specs, check_vma=False)
```

time: 535 us -> 77.3 us (0.14)
  the two profiles are of different devices: /device:TPU:0 before, /device:TPU:1 now
where the time goes in v1:
time: 77.3 us; the launch traced here: 77 us
  Pallas kernels  66.6 us (86%)
  local copies, waits for them, and re-layouts  9.75 us (13%)
    pallas_call x1, Pallas kernels, shards(): pl.pallas_call(kernel, out_shape=(jax.ShapeDtypeStruct((V, ROWS, XN), F32...  66.6 us
    unnamed x17, local copies, waits for them, and re-layouts  9.75 us

profile of v1, /device:TPU:1, one launch (start us, length us, event | category | flops | bytes accessed | tf_op | source)
XLA Modules:
  0.0 77.0 jit_solution(15750189439979005865)
XLA Ops:
  0.6 0.0 copy-start
  0.6 1.6 %copy-done = f32[16,64,4,128]{3,2,1,0:T(4,128)S(1)} copy-done((f32[16,64,4,128]{3,2,1,0:T(4,128)S(1)}, f32[16,64,4,128]{3,2,1,0:T(4,128)}, u32[]{:S(2)}) %copy-start) | copy-done | bytes 2097176
  2.2 0.0 copy-start.1
  2.2 1.6 %copy-done.1 = f32[16,64,4,128]{3,2,1,0:T(4,128)S(1)} copy-done((f32[16,64,4,128]{3,2,1,0:T(4,128)S(1)}, f32[16,64,4,128]{3,2,1,0:T(4,128)}, u32[]{:S(2)}) %copy-start.1) | copy-done | bytes 2097176
  3.8 0.0 copy-start.2
  3.8 1.0 %copy-done.2 = f32[3,64,4,128]{3,2,1,0:T(4,128)S(1)} copy-done((f32[3,64,4,128]{3,2,1,0:T(4,128)S(1)}, f32[3,64,4,128]{3,2,1,0:T(4,128)}, u32[]{:S(2)}) %copy-start.2) | copy-done | bytes 393240
  4.8 0.0 copy-start.3
  4.8 0.8 %copy-done.3 = bf16[512,64]{0,1:T(8,128)(2,1)S(1)} copy-done((bf16[512,64]{0,1:T(8,128)(2,1)S(1)}, bf16[512,64]{0,1:T(8,128)(2,1)}, u32[]{:S(2)}) %copy-start.3) | copy-done | bytes 65560
  5.7 0.0 copy-start.4
  5.7 0.8 %copy-done.4 = f32[256,64]{0,1:T(8,128)S(1)} copy-done((f32[256,64]{0,1:T(8,128)S(1)}, f32[256,64]{0,1:T(8,128)}, u32[]{:S(2)}) %copy-start.4) | copy-done | bytes 65560
  6.5 0.0 copy-start.5
  6.5 0.7 copy-done.5
  7.2 0.0 copy-start.6
  7.2 0.7 copy-done.6
  7.8 66.6 %section.1 = (f32[16,256,128]{2,1,0:T(8,128)S(1)}, f32[8,512]{1,0:T(8,128)S(1)}, f32[64,256]{1,0:T(8,128)S(1)}) custom-call(f32[16]{0:T(128)S(1)} %copy-done.6, f32[16,16]{1,0:T(8,128)S(1)} %copy-done.5, bf16[64,512]{1,0:T(8,128)(2,1)S(1)} %bitcast.13, f32[64,256]{1,0:T(8,128)S(1)} %bitcast.14, f32[16,256,128]{2,1,0:T(8,128)S(1)} %bitcast.9, ...), custom_call_target="tpu_custom_call" | custom-call | tf_op jit(solution)/shard_map/section/pallas_call | solution.py:509
  74.5 1.3 %copy.13 = f32[16,64,4,128]{3,2,1,0:T(4,128)} copy(f32[16,64,4,128]{3,2,1,0:T(4,128)S(1)} %bitcast.11) | data formatting | bytes 4194304
  75.8 0.6 copy.14
  76.4 0.6 copy.15
Async XLA Ops:
  0.6 1.6 %copy-start = (f32[16,64,4,128]{3,2,1,0:T(4,128)S(1)}, f32[16,64,4,128]{3,2,1,0:T(4,128)}, u32[]{:S(2)}) copy-start(f32[16,64,4,128]{3,2,1,0:T(4,128)} %param.7) | copy-start | bytes 6291460
  2.2 1.6 %copy-start.1 = (f32[16,64,4,128]{3,2,1,0:T(4,128)S(1)}, f32[16,64,4,128]{3,2,1,0:T(4,128)}, u32[]{:S(2)}) copy-start(f32[16,64,4,128]{3,2,1,0:T(4,128)} %param.8) | copy-start | bytes 6291460
  3.8 1.0 %copy-start.2 = (f32[3,64,4,128]{3,2,1,0:T(4,128)S(1)}, f32[3,64,4,128]{3,2,1,0:T(4,128)}, u32[]{:S(2)}) copy-start(f32[3,64,4,128]{3,2,1,0:T(4,128)} %param.9) | copy-start | bytes 1179652
  4.8 0.8 %copy-start.3 = (bf16[512,64]{0,1:T(8,128)(2,1)S(1)}, bf16[512,64]{0,1:T(8,128)(2,1)}, u32[]{:S(2)}) copy-start(bf16[512,64]{0,1:T(8,128)(2,1)} %param.12) | copy-start | bytes 196612
  5.7 0.8 %copy-start.4 = (f32[256,64]{0,1:T(8,128)S(1)}, f32[256,64]{0,1:T(8,128)}, u32[]{:S(2)}) copy-start(f32[256,64]{0,1:T(8,128)} %param.13) | copy-start | bytes 196612
  6.5 0.7 copy-start.5
  7.2 0.7 copy-start.6

commit v2 on v1

--- a/solution.py
+++ b/solution.py
@@ -30,11 +30,11 @@
 
 
 def kernel(
-    dif, rea, xft, yft, fields, start, vel,
+    dif_in, rea_in, xft_in, yft_in, fields, start, vel,
     new_out, gram_out, yprod_out,
-    fbuf, sbuf, vbuf, obuf, zsend, zrecv, xpack, xrecv, xcomb, snap, full, kmat, rfb,
+    dif, rea, xft, yft, fbuf, sbuf, vbuf, zsend, zrecv, xpack, xrecv, xcomb, snap, full, kmat, rfb,
     gacc, r1, g2, r2, s2, r3, pbuf, mbuf, ysend, yrecv,
-    load_sem, out_sem, zs_sem, zr_sem, ys_sem, yr_sem, xs_sem, xr_sem, as_sem, ar_sem,
+    load_sem, zs_sem, zr_sem, ys_sem, yr_sem, xs_sem, xr_sem, as_sem, ar_sem,
     ps_sem, pr_sem, bs_sem, br_sem, s1_sem, r1_sem, s2_sem, r2_sem, s3_sem, r3_sem,
 ):
     gy, gz, ga = lax.axis_index("gy"), lax.axis_index("gz"), lax.axis_index("ga")
@@ -54,9 +54,16 @@
     load_f = pltpu.make_async_copy(fields, fbuf.at[:, pl.ds(PAD, ROWS), :], load_sem.at[0])
     load_s = pltpu.make_async_copy(start, sbuf, load_sem.at[1])
     load_v = pltpu.make_async_copy(vel, vbuf, load_sem.at[2])
+    load_small = [
+        pltpu.make_async_copy(src, dst, load_sem.at[3 + i])
+        for i, (src, dst) in enumerate(((rea_in, rea), (dif_in, dif), (xft_in, xft), (yft_in, yft)))
+    ]
     load_f.start()
+    load_small[0].start()
     load_s.start()
     load_v.start()
+    for copy in load_small[1:]:
+        copy.start()
 
     barrier = pltpu.get_barrier_semaphore()
     wrap_up = jnp.logical_and(cz == 3, gz < NZ - 1)
@@ -96,6 +103,8 @@
     @pl.when(ga == 0)
     def _():
         xrecv[0] = jnp.zeros((YN, XN), F32)
+
+    load_small[0].wait()
 
     low16 = lax.broadcasted_iota(jnp.int32, (V * YC, V), 0) // YC
     spread = (low16 == lax.broadcasted_iota(jnp.int32, (V * YC, V), 1)).astype(F32).astype(BF16)
@@ -195,24 +204,21 @@
         slab = (ga + j) % NA
         return bring(snap.at[c, slab], full.at[c, slab], as_sem.at[c, j], ar_sem.at[c, slab], (gy, gz, slab))
 
-    def store_out(c):
-        rows = pl.ds(c * CR, CR)
-        return pltpu.make_async_copy(obuf.at[:, rows, :], new_out.at[:, rows, :], out_sem.at[c])
-
     def hand_over(c):
         full[c, ga] = snap[c, ga]
         for j in (2, 3, 1):
             exchange(c, j).start()
-        store_out(c).start()
 
     load_s.wait()
     load_v.wait()
+    for copy in load_small[1:]:
+        copy.wait()
 
     @pl.when(buffer_slab)
     def _():
         def chunk(c, carry):
             def variable(v, inner):
-                obuf[v, pl.ds(c * CR, CR), :] = fbuf[v, pl.ds(PAD + c * CR, CR), :]
+                new_out[v, pl.ds(c * CR, CR), :] = fbuf[v, pl.ds(PAD + c * CR, CR), :]
                 for z in range(ZN):
                     piece = fbuf[v, pl.ds(PAD + c * CR + z, YC, stride=ZN), :]
                     snap[c, z, v] = piece.astype(BF16)
@@ -295,7 +301,7 @@
                         0.75 * began + 0.25 * here
                         + ((0.25 * time_step) * dif[v]) * laplace - advection + rfb[v]
                     )
-                    obuf[v, pl.ds(c * CR + z, YC, stride=ZN), :] = value
+                    new_out[v, pl.ds(c * CR + z, YC, stride=ZN), :] = value
                     snap[c, z, v] = value.astype(BF16)
                     return inner
 
@@ -456,7 +462,6 @@
     def sent(c, carry):
         for j in range(1, NA):
             exchange(c, j).wait_send()
-        store_out(c).wait()
 
         @pl.when(jnp.logical_not(diagonal))
         def _():
@@ -502,24 +507,38 @@
     lax.fori_loop(1, 16, column_sent, 0)
 
 
+def finish(new, gram, product, new_out, gram_out, product_out, sem):
+    copies = [
+        pltpu.make_async_copy(src, dst, sem.at[i])
+        for i, (src, dst) in enumerate(((new, new_out), (gram, gram_out), (product, product_out)))
+    ]
+    for copy in copies:
+        copy.start()
+    for copy in copies:
+        copy.wait()
+
+
 def shards(fields, section_start, velocity, diffusivity, reaction, x_factor, y_factor):
     vmem = pl.BlockSpec(memory_space=pltpu.VMEM)
-    hbm = pl.BlockSpec(memory_space=pl.ANY)
+    hbm = pl.BlockSpec(memory_space=pltpu.HBM)
     dma = pltpu.SemaphoreType.DMA
     new_fields, gram, product = pl.pallas_call(
         kernel,
         out_shape=(
-            jax.ShapeDtypeStruct((V, ROWS, XN), F32),
-            jax.ShapeDtypeStruct((8, 512), F32),
-            jax.ShapeDtypeStruct((64, 256), F32),
+            pltpu.VMEM((V, ROWS, XN), F32),
+            pltpu.VMEM((8, 512), F32),
+            pltpu.VMEM((64, 256), F32),
         ),
-        in_specs=[pl.BlockSpec(memory_space=pltpu.SMEM), vmem, vmem, vmem, hbm, hbm, hbm],
-        out_specs=(hbm, vmem, vmem),
+        in_specs=[hbm] * 7,
+        out_specs=(vmem, vmem, vmem),
         scratch_shapes=[
+            pltpu.SMEM((V,), F32),
+            pltpu.VMEM((V, V), F32),
+            pltpu.VMEM((64, 512), BF16),
+            pltpu.VMEM((64, 256), F32),
             pltpu.VMEM((V, PAD + ROWS + PAD, XN), F32),
             pltpu.VMEM((V, ROWS, XN), F32),
             pltpu.VMEM((3, ROWS, XN), F32),
-            pltpu.VMEM((V, ROWS, XN), F32),
             pltpu.VMEM((2, NC, V, YC, XN), BF16),
             pltpu.VMEM((2, NC, V, YC, XN), BF16),
             pltpu.VMEM((YN, XN), F32),
@@ -539,25 +558,42 @@
             pltpu.VMEM((V // 2, 16, YC, XN), BF16),
             pltpu.VMEM((64, 256), F32),
             pltpu.VMEM((64, 256), F32),
-            dma((3,)), dma((NC,)),
+            dma((7,)),
             dma((2, NC)), dma((2, NC)), dma((2,)), dma((2,)), dma((2,)), dma((2,)),
             dma((NC, NA)), dma((NC, NA)),
             dma((NC,)), dma((16,)), dma((NA,)), dma,
             dma, dma, dma((16,)), dma((16,)), dma((16,)), dma((16,)),
         ],
         compiler_params=pltpu.CompilerParams(
-            collective_id=0, has_side_effects=True, vmem_limit_bytes=40 << 20
+            collective_id=0, has_side_effects=True, vmem_limit_bytes=24 << 20
         ),
         name="section",
     )(
-        diffusivity,
-        reaction,
-        x_factor.T,
-        y_factor.T,
-        fields.reshape(V, ROWS, XN),
-        section_start.reshape(V, ROWS, XN),
-        velocity.reshape(3, ROWS, XN),
+        *(
+            pltpu.with_memory_space_constraint(array, pltpu.HBM)
+            for array in (
+                diffusivity,
+                reaction,
+                x_factor.T,
+                y_factor.T,
+                fields.reshape(V, ROWS, XN),
+                section_start.reshape(V, ROWS, XN),
+                velocity.reshape(3, ROWS, XN),
+            )
+        )
     )
+    new_fields, gram, product = pl.pallas_call(
+        finish,
+        out_shape=(
+            jax.ShapeDtypeStruct((V, ROWS, XN), F32),
+            jax.ShapeDtypeStruct((8, 512), F32),
+            jax.ShapeDtypeStruct((64, 256), F32),
+        ),
+        in_specs=[pl.BlockSpec(memory_space=pl.ANY)] * 3,
+        out_specs=(hbm,) * 3,
+        scratch_shapes=[dma((3,))],
+        name="finish", compiler_params=pltpu.CompilerParams(vmem_limit_bytes=1 << 20),
+    )(new_fields, gram, product)
     return new_fields.reshape(V, YN, ZN, XN), gram, product.T[None]
 
 

time: 77.3 us -> 67.7 us (0.88)
  local copies, waits for them, and re-layouts: 9.75 us -> 0 us
    unnamed x17 -> x0, local copies, waits for them, and re-layouts: 9.75 us -> none
    pallas_call x1 -> x2, Pallas kernels: 66.6 us -> 67 us  [the longest x1 65.7 us: shards(): pl.pallas_call(kernel, out_shape=(pltpu.VMEM((V, ROWS, XN), F32), pltpu.V...]
where the time goes in v2:
time: 67.7 us
  Pallas kernels  67 us (99%)
    pallas_call x1, Pallas kernels, shards(): pl.pallas_call(kernel, out_shape=(pltpu.VMEM((V, ROWS, XN), F32), pltpu.V...  65.7 us

profile of v2, /device:TPU:1, one launch (start us, length us, event | category | flops | bytes accessed | tf_op | source)
XLA Modules:
  0.0 67.7 jit_solution(3032760691718086471)
XLA Ops:
  0.6 65.7 %section.1 = (f32[16,256,128]{2,1,0:T(8,128)S(1)}, f32[8,512]{1,0:T(8,128)S(1)}, f32[64,256]{1,0:T(8,128)S(1)}) custom-call(f32[16]{0:T(128)} %dif_in.1, f32[16,16]{1,0:T(8,128)} %rea_in.1, bf16[64,512]{1,0:T(8,128)(2,1)} %bitcast.12, f32[64,256]{1,0:T(8,128)} %bitcast.13, f32[16,256,128]{2,1,0:T(8,128)} %bitcast.9, f32[16,256,128]{2,1,0:T(8,128)} %bitcast.10, ...), custom_call_target="tpu_custom_call" | custom-call | tf_op jit(solution)/shard_map/section/pallas_call | solution.py:525
  66.3 1.4 %finish.1 = (f32[16,256,128]{2,1,0:T(8,128)}, f32[8,512]{1,0:T(8,128)}, f32[64,256]{1,0:T(8,128)}) custom-call(f32[16,256,128]{2,1,0:T(8,128)S(1)} %get-tuple-element.9.new, f32[8,512]{1,0:T(8,128)S(1)} %get-tuple-element.10.gram, f32[64,256]{1,0:T(8,128)S(1)} %get-tuple-element.11.product), custom_call_target="tpu_custom_call" | custom-call | tf_op jit(solution)/shard_map/finish/pallas_call | solution.py:585

commit v3 on v2

--- a/solution.py
+++ b/solution.py
@@ -43,6 +43,11 @@
     plane = gy * 4 + cy
     column = (zhi * 4 + cz) * 2 + core
     buffer_slab = ga == NA - 1
+    first_chip = zhi == 0
+    second_chip = zhi == 1
+    diagonal = gy == ga
+    to_second = jnp.logical_and(first_chip, gy != ga + 2)
+    from_first = jnp.logical_and(second_chip, diagonal)
     inner_slab = ga < NA - 1
 
     def plane_device(index):
@@ -82,7 +87,17 @@
         pl.semaphore_signal(barrier, inc=1, device_id=column_device((column + j) % 16), device_id_type=MESH)
         return carry
 
-    lax.fori_loop(1, 16, greet, 0)
+    for j in range(1, 16):
+        greet(j, 0)
+
+    @pl.when(to_second)
+    def _():
+        pl.semaphore_signal(barrier, inc=1, device_id=(ga + 2, gz, ga + 2), device_id_type=MESH)
+
+    @pl.when(from_first)
+    def _():
+        for j in range(1, NY):
+            pl.semaphore_signal(barrier, inc=1, device_id=((gy + j) % NY, gz, ga - 2), device_id_type=MESH)
 
     @pl.when(gy == 0)
     def _():
@@ -103,6 +118,147 @@
     @pl.when(ga == 0)
     def _():
         xrecv[0] = jnp.zeros((YN, XN), F32)
+
+    load_f.wait()
+
+    @pl.when(inner_slab)
+    def _():
+        def face(v, carry):
+            for side, z in ((0, 0), (1, ZN - 1)):
+                for c in range(NC):
+                    piece = fbuf[v, pl.ds(PAD + c * CR + z, YC, stride=ZN), :]
+                    zsend[side, c, v] = piece.astype(BF16)
+            return carry
+
+        lax.fori_loop(0, V, face, 0)
+
+    pl.semaphore_wait(
+        barrier,
+        30 + wrap_up.astype(jnp.int32) + wrap_down.astype(jnp.int32)
+        + to_second.astype(jnp.int32) + 3 * from_first.astype(jnp.int32),
+    )
+
+    def z_copy(side, c):
+        return bring(
+            zsend.at[side, c], zrecv.at[1 - side, c], zs_sem.at[side, c], zr_sem.at[1 - side, c],
+            (gy, gz - 1 + 2 * side, ga),
+        )
+
+    low_z = jnp.logical_and(inner_slab, gz > 0)
+    high_z = jnp.logical_and(inner_slab, gz < NZ - 1)
+    low_y = jnp.logical_and(inner_slab, gy > 0)
+    high_y = jnp.logical_and(inner_slab, gy < NY - 1)
+
+    def y_copy(side):
+        src = fields.at[:, pl.ds((ROWS - PAD) * side, PAD), :]
+        dst = fbuf.at[:, pl.ds((PAD + ROWS) * (1 - side), PAD), :]
+        return bring(src, dst, ys_sem.at[side], yr_sem.at[1 - side], (gy - 1 + 2 * side, gz, ga))
+
+    def start_faces(c):
+        @pl.when(low_z)
+        def _():
+            z_copy(0, c).start()
+
+        @pl.when(high_z)
+        def _():
+            z_copy(1, c).start()
+
+    def faces_sent(c):
+        @pl.when(low_z)
+        def _():
+            z_copy(0, c).wait_send()
+
+        @pl.when(high_z)
+        def _():
+            z_copy(1, c).wait_send()
+
+    start_faces(0)
+
+    @pl.when(low_y)
+    def _():
+        y_copy(0).start()
+
+    @pl.when(high_y)
+    def _():
+        y_copy(1).start()
+
+    lane = lax.broadcasted_iota(jnp.int32, (YN, XN), 1)
+
+    def pack(v, acc):
+        for z in range(ZN):
+            at = 2 * (v * ZN + z)
+            piece = fbuf[v, pl.ds(PAD + z, YN, stride=ZN), :]
+            moved = pltpu.roll(piece, at + 1, 1)
+            acc = jnp.where(jnp.logical_or(lane == at, lane == at + 1), moved, acc)
+        return acc
+
+    xpack[...] = lax.fori_loop(0, V, pack, jnp.zeros((YN, XN), F32))
+
+    def x_copy(side):
+        return bring(
+            xpack, xrecv.at[1 - side], xs_sem.at[side], xr_sem.at[1 - side], (gy, gz, ga - 1 + 2 * side)
+        )
+
+    low_x = ga > 0
+    high_x = ga < NA - 2
+
+    @pl.when(low_x)
+    def _():
+        x_copy(0).start()
+
+    @pl.when(high_x)
+    def _():
+        x_copy(1).start()
+
+    for c in range(1, NC):
+        start_faces(c)
+
+    def exchange(c, j):
+        peer = (ga + j) % NA
+        return bring(snap.at[c, peer], full.at[c, ga], as_sem.at[c, j], ar_sem.at[c, ga], (gy, gz, peer))
+
+    def arrived(c, j):
+        slab = (ga + j) % NA
+        return bring(snap.at[c, slab], full.at[c, slab], as_sem.at[c, j], ar_sem.at[c, slab], (gy, gz, slab))
+
+    last = NC - 1
+
+    def last_exchange(layer):
+        return bring(
+            snap.at[last, layer], full.at[last + layer // 2, ga], as_sem.at[last, layer],
+            ar_sem.at[last + layer // 2, ga], (gy, gz, layer % 2),
+        )
+
+    def last_swap(m):
+        return bring(
+            snap.at[last, 2 * m + 1 - core], full.at[last + m, ga], as_sem.at[last, m],
+            ar_sem.at[last + m, ga], (gy, gz, 1 - core),
+        )
+
+    def last_arrived(block, j):
+        slab = (ga + j) % NA
+        return bring(
+            snap.at[0, slab], full.at[block, slab], as_sem.at[0, j], ar_sem.at[block, slab], (gy, gz, slab)
+        )
+
+    def hand_over(c):
+        @pl.when(c < last)
+        def _():
+            full[c, ga] = snap[c, ga]
+            for j in (2, 3, 1):
+                exchange(c, j).start()
+
+        @pl.when(jnp.logical_and(c == last, first_chip))
+        def _():
+            for m in range(2):
+                last_swap(m).start()
+            for m in range(2):
+                full[last + m, ga] = snap[last, 2 * m + core]
+
+        @pl.when(jnp.logical_and(c == last, second_chip))
+        def _():
+            for layer in range(NA):
+                last_exchange(layer).start()
 
     load_small[0].wait()
 
@@ -114,100 +270,10 @@
     rate = (0.25 * time_step) * rea[...]
     rate_high = rate.astype(BF16)
     rate_low = (rate - rate_high.astype(F32)).astype(BF16)
-    for part, piece in enumerate((rate_high, rate_low)):
+    for part, piece in enumerate((rate_high, rate_high, rate_low)):
         tall = jnp.dot(spread, piece, preferred_element_type=F32).astype(BF16)
         square = lax.dot_general(tall, spread, (((1,), (1,)), ((), ())), preferred_element_type=F32)
-        kmat[part] = jnp.where(same, square, 0.0).astype(BF16)
-
-    load_f.wait()
-
-    @pl.when(inner_slab)
-    def _():
-        def face(v, carry):
-            for side, z in ((0, 0), (1, ZN - 1)):
-                for c in range(NC):
-                    piece = fbuf[v, pl.ds(PAD + c * CR + z, YC, stride=ZN), :]
-                    zsend[side, c, v] = piece.astype(BF16)
-            return carry
-
-        lax.fori_loop(0, V, face, 0)
-
-    pl.semaphore_wait(barrier, 30 + wrap_up.astype(jnp.int32) + wrap_down.astype(jnp.int32))
-
-    def z_copy(side, c):
-        return bring(
-            zsend.at[side, c], zrecv.at[1 - side, c], zs_sem.at[side, c], zr_sem.at[1 - side, c],
-            (gy, gz - 1 + 2 * side, ga),
-        )
-
-    low_z = jnp.logical_and(inner_slab, gz > 0)
-    high_z = jnp.logical_and(inner_slab, gz < NZ - 1)
-    low_y = jnp.logical_and(inner_slab, gy > 0)
-    high_y = jnp.logical_and(inner_slab, gy < NY - 1)
-
-    def y_copy(side):
-        src = fields.at[:, pl.ds((ROWS - PAD) * side, PAD), :]
-        dst = fbuf.at[:, pl.ds((PAD + ROWS) * (1 - side), PAD), :]
-        return bring(src, dst, ys_sem.at[side], yr_sem.at[1 - side], (gy - 1 + 2 * side, gz, ga))
-
-    for c in range(NC):
-        @pl.when(low_z)
-        def _():
-            z_copy(0, c).start()
-
-        @pl.when(high_z)
-        def _():
-            z_copy(1, c).start()
-
-        if c == 0:
-            @pl.when(low_y)
-            def _():
-                y_copy(0).start()
-
-            @pl.when(high_y)
-            def _():
-                y_copy(1).start()
-
-    lane = lax.broadcasted_iota(jnp.int32, (YN, XN), 1)
-
-    def pack(v, acc):
-        for z in range(ZN):
-            at = 2 * (v * ZN + z)
-            piece = fbuf[v, pl.ds(PAD + z, YN, stride=ZN), :]
-            moved = pltpu.roll(piece, at + 1, 1)
-            acc = jnp.where(jnp.logical_or(lane == at, lane == at + 1), moved, acc)
-        return acc
-
-    xpack[...] = lax.fori_loop(0, V, pack, jnp.zeros((YN, XN), F32))
-
-    def x_copy(side):
-        return bring(
-            xpack, xrecv.at[1 - side], xs_sem.at[side], xr_sem.at[1 - side], (gy, gz, ga - 1 + 2 * side)
-        )
-
-    low_x = ga > 0
-    high_x = ga < NA - 2
-
-    @pl.when(low_x)
-    def _():
-        x_copy(0).start()
-
-    @pl.when(high_x)
-    def _():
-        x_copy(1).start()
-
-    def exchange(c, j):
-        peer = (ga + j) % NA
-        return bring(snap.at[c, peer], full.at[c, ga], as_sem.at[c, j], ar_sem.at[c, ga], (gy, gz, peer))
-
-    def arrived(c, j):
-        slab = (ga + j) % NA
-        return bring(snap.at[c, slab], full.at[c, slab], as_sem.at[c, j], ar_sem.at[c, slab], (gy, gz, slab))
-
-    def hand_over(c):
-        full[c, ga] = snap[c, ga]
-        for j in (2, 3, 1):
-            exchange(c, j).start()
+        kmat[:, V * YC * part : V * YC * (part + 1)] = jnp.where(same, square, 0.0).astype(BF16)
 
     load_s.wait()
     load_v.wait()
@@ -257,6 +323,8 @@
             def _():
                 z_copy(0, c).wait_recv()
 
+            faces_sent(c)
+
             for z in range(ZN):
                 first = PAD + c * CR + z
                 stack = jnp.concatenate(
@@ -264,10 +332,8 @@
                 )
                 high = stack.astype(BF16)
                 low = (stack - high.astype(F32)).astype(BF16)
-                reacted = (
-                    jnp.dot(kmat[0], high, preferred_element_type=F32)
-                    + jnp.dot(kmat[0], low, preferred_element_type=F32)
-                    + jnp.dot(kmat[1], high, preferred_element_type=F32)
+                reacted = jnp.dot(
+                    kmat[...], jnp.concatenate([high, low, high], axis=0), preferred_element_type=F32
                 )
                 rfb[...] = reacted.reshape(V, YC, XN)
                 scale = 0.125 * time_step
@@ -311,13 +377,9 @@
 
         lax.fori_loop(0, NC, chunk, 0)
 
-    diagonal = gy == ga
-    diagonal_device = (ga, gz, ga)
-
-    def project_copy(c):
-        return bring(
-            pbuf.at[c], mbuf.at[:, gy * NC + c], ps_sem.at[c], pr_sem.at[gy * NC + c], diagonal_device
-        )
+    def project_copy(block, layer):
+        slot = gy * NC + jnp.minimum(block, last)
+        return bring(pbuf.at[block], mbuf.at[:, slot], ps_sem.at[block], pr_sem.at[slot], (layer, gz, layer))
 
     zero = jnp.zeros_like(xft[...])
     first_half = jnp.concatenate([xft[...], zero], axis=0)
@@ -325,49 +387,72 @@
     nt = (((1,), (1,)), ((), ()))
     tn = (((0,), (0,)), ((), ()))
 
+    def project(block):
+        wide = jnp.concatenate([full[block, s].reshape(V * YC, XN) for s in range(NA)], axis=1)
+        rows = V * YC // 2
+        projected = lax.dot_general(wide[:rows], first_half, nt, preferred_element_type=F32)
+        projected += lax.dot_general(wide[rows:], second_half, nt, preferred_element_type=F32)
+        return wide, projected.astype(BF16).reshape(V // 2, YC, XN)
+
+    def add_gram(block, wide, begin):
+        for i in range(2):
+            half = (core + 1 + i) % 2
+            part = jnp.concatenate(
+                [full[block, 2 * half + s].reshape(V * YC, XN) for s in range(2)], axis=1
+            )
+            term = lax.dot_general(wide, part, tn, preferred_element_type=F32)
+
+            @pl.when(begin)
+            def _():
+                gacc[i] = term
+
+            @pl.when(jnp.logical_not(begin))
+            def _():
+                gacc[i] = gacc[i] + term
+
+    def own_layer(block, projected):
+        @pl.when(diagonal)
+        def _():
+            mbuf[:, gy * NC + block] = projected
+
+        @pl.when(jnp.logical_not(diagonal))
+        def _():
+            pbuf[block] = projected
+            project_copy(block, ga).start()
+
     def gather_gram(c, carry):
         for j in range(1, NA):
             arrived(c, j).wait_recv()
-        wide = jnp.concatenate([full[c, s].reshape(V * YC, XN) for s in range(NA)], axis=1)
-        for i in range(2):
-            half = (core + 1 + i) % 2
-            part = jnp.concatenate(
-                [full[c, 2 * half + s].reshape(V * YC, XN) for s in range(2)], axis=1
-            )
-            term = lax.dot_general(wide, part, tn, preferred_element_type=F32)
-
-            @pl.when(c == 0)
+        wide, projected = project(c)
+        own_layer(c, projected)
+        add_gram(c, wide, c == 0)
+        return carry
+
+    lax.fori_loop(0, last, gather_gram, 0)
+
+    @pl.when(first_chip)
+    def _():
+        def extra(block, carry):
+            for j in range(1, NA):
+                last_arrived(block, j).wait_recv()
+            wide, projected = project(block)
+
+            @pl.when(block == last)
             def _():
-                gacc[i] = term
-
-            @pl.when(c > 0)
+                own_layer(block, projected)
+
+            @pl.when(block == NC)
             def _():
-                gacc[i] = gacc[i] + term
-
-            if i == 0:
-                @pl.when(c == NC - 1)
-                def _():
-                    bring(gacc.at[0], r1, s1_sem, r1_sem, (gy, gz, zhi * 2 + 1 - core)).start()
-
-        rows = V * YC // 2
-        projected = lax.dot_general(wide[:rows], first_half, nt, preferred_element_type=F32)
-        projected += lax.dot_general(wide[rows:], second_half, nt, preferred_element_type=F32)
-        projected = projected.astype(BF16).reshape(V // 2, YC, XN)
-
-        @pl.when(diagonal)
-        def _():
-            mbuf[:, gy * NC + c] = projected
-
-        @pl.when(jnp.logical_not(diagonal))
-        def _():
-            pbuf[c] = projected
-            project_copy(c).start()
-
-        return carry
-
-    lax.fori_loop(0, NC, gather_gram, 0)
+                pbuf[block] = projected
+                project_copy(block, ga + 2).start()
+
+            add_gram(block, wide, block < 0)
+            return carry
+
+        lax.fori_loop(last, NC + 1, extra, 0)
 
     pair = bring(gacc.at[0], r1, s1_sem, r1_sem, (gy, gz, zhi * 2 + 1 - core))
+    pair.start()
     pair.wait_recv()
     g2[...] = (gacc[1] + r1[...]).astype(BF16).reshape(16, 32, 256)
 
@@ -383,7 +468,8 @@
         plane_copy(j).start()
         return carry
 
-    lax.fori_loop(1, 16, start_plane, 0)
+    for j in range(1, 16):
+        start_plane(j, 0)
 
     def bcast_copy(j):
         peer = (ga + j) % NA
@@ -392,13 +478,17 @@
     @pl.when(diagonal)
     def _():
         def wait_projected(i, carry):
-            slot = (gy * NC + NC + i) % 16
+            slot = (gy * NC + i) % 16
             bring(
-                pbuf.at[0], mbuf.at[:, slot], ps_sem.at[0], pr_sem.at[slot], diagonal_device
+                pbuf.at[0], mbuf.at[:, slot], ps_sem.at[0], pr_sem.at[slot], ((ga + 1) % NA, gz, ga)
             ).wait_recv()
             return carry
 
-        lax.fori_loop(0, 3 * NC, wait_projected, 0)
+        @pl.when(second_chip)
+        def _():
+            wait_projected(last, 0)
+
+        lax.fori_loop(NC, 16, wait_projected, 0)
         y_gram = jnp.zeros((256, 256), F32)
         for i in range(V // 2):
             layer = mbuf[i].reshape(256, XN)
@@ -415,7 +505,9 @@
         plane_arrived(j).wait_recv()
         return acc + r2[(plane + j) % 16].astype(F32)
 
-    total = lax.fori_loop(1, 16, add_plane, g2[plane].astype(F32))
+    total = g2[plane].astype(F32)
+    for j in range(1, 16):
+        total = add_plane(j, total)
     s2[...] = total.reshape(4, 8, 256)
     r3[column] = s2[cz]
 
@@ -431,17 +523,8 @@
         column_copy(j).start()
         return carry
 
-    lax.fori_loop(1, 16, start_column, 0)
-
-    @pl.when(low_z)
-    def _():
-        for c in range(NC):
-            z_copy(0, c).wait_send()
-
-    @pl.when(high_z)
-    def _():
-        for c in range(NC):
-            z_copy(1, c).wait_send()
+    for j in range(1, 16):
+        start_column(j, 0)
 
     @pl.when(low_y)
     def _():
@@ -465,18 +548,36 @@
 
         @pl.when(jnp.logical_not(diagonal))
         def _():
-            project_copy(c).wait_send()
+            project_copy(c, ga).wait_send()
 
         return carry
 
-    lax.fori_loop(0, NC, sent, 0)
+    lax.fori_loop(0, last, sent, 0)
+
+    @pl.when(first_chip)
+    def _():
+        for m in range(2):
+            last_swap(m).wait_send()
+
+        @pl.when(jnp.logical_not(diagonal))
+        def _():
+            project_copy(last, ga).wait_send()
+
+        project_copy(NC, ga + 2).wait_send()
+
+    @pl.when(second_chip)
+    def _():
+        for layer in range(NA):
+            last_exchange(layer).wait_send()
+
     pair.wait_send()
 
     def plane_sent(j, carry):
         plane_copy(j).wait_send()
         return carry
 
-    lax.fori_loop(1, 16, plane_sent, 0)
+    for j in range(1, 16):
+        plane_sent(j, 0)
 
     @pl.when(diagonal)
     def _():
@@ -492,7 +593,8 @@
         column_arrived(j).wait_recv()
         return carry
 
-    lax.fori_loop(1, 16, column_wait, 0)
+    for j in range(1, 16):
+        column_wait(j, 0)
     cells = 1.0 / float(V * 256 * 64)
     for half in range(2):
         acc = r3[half]
@@ -504,7 +606,8 @@
         column_copy(j).wait_send()
         return carry
 
-    lax.fori_loop(1, 16, column_sent, 0)
+    for j in range(1, 16):
+        column_sent(j, 0)
 
 
 def finish(new, gram, product, new_out, gram_out, product_out, sem):
@@ -545,8 +648,8 @@
             pltpu.VMEM((2, YN, XN), F32),
             pltpu.VMEM((YN, XN), F32),
             pltpu.VMEM((NC, ZN, V, YC, XN), BF16),
-            pltpu.VMEM((NC, NA, V, YC, XN), BF16),
-            pltpu.VMEM((2, V * YC, V * YC), BF16),
+            pltpu.VMEM((NC + 1, NA, V, YC, XN), BF16),
+            pltpu.VMEM((V * YC, 3 * V * YC), BF16),
             pltpu.VMEM((V, YC, XN), F32),
             pltpu.VMEM((2, 512, 256), F32),
             pltpu.VMEM((512, 256), F32),
@@ -554,14 +657,14 @@
             pltpu.VMEM((16, 32, 256), BF16),
             pltpu.VMEM((4, 8, 256), F32),
             pltpu.VMEM((16, 8, 256), F32),
-            pltpu.VMEM((NC, V // 2, YC, XN), BF16),
+            pltpu.VMEM((NC + 1, V // 2, YC, XN), BF16),
             pltpu.VMEM((V // 2, 16, YC, XN), BF16),
             pltpu.VMEM((64, 256), F32),
             pltpu.VMEM((64, 256), F32),
             dma((7,)),
             dma((2, NC)), dma((2, NC)), dma((2,)), dma((2,)), dma((2,)), dma((2,)),
-            dma((NC, NA)), dma((NC, NA)),
-            dma((NC,)), dma((16,)), dma((NA,)), dma,
+            dma((NC, NA)), dma((NC + 1, NA)),
+            dma((NC + 1,)), dma((16,)), dma((NA,)), dma,
             dma, dma, dma((16,)), dma((16,)), dma((16,)), dma((16,)),
         ],
         compiler_params=pltpu.CompilerParams(

time: 67.7 us -> 65.6 us (0.969)
  Pallas kernels: 67 us -> 64.8 us
    pallas_call x1, Pallas kernels: 65.7 us -> 63.5 us  [shards(): pl.pallas_call(kernel, out_shape=(pltpu.VMEM((V, ROWS, XN), F32), pltpu.V...]
where the time goes in v3:
time: 65.6 us; the launch traced here: 65.5 us
  Pallas kernels  64.8 us (99%)
    pallas_call x1, Pallas kernels, shards(): pl.pallas_call(kernel, out_shape=(pltpu.VMEM((V, ROWS, XN), F32), pltpu.V...  63.5 us
    pallas_call x1, Pallas kernels, shards(): pl.pallas_call(finish, out_shape=(jax.ShapeDtypeStruct((V, ROWS, XN), F32...  1.35 us

profile of v3, /device:TPU:1, one launch (start us, length us, event | category | flops | bytes accessed | tf_op | source)
XLA Modules:
  0.0 65.5 jit_solution(240164708565942279)
XLA Ops:
  0.6 63.5 %section.1 = (f32[16,256,128]{2,1,0:T(8,128)S(1)}, f32[8,512]{1,0:T(8,128)S(1)}, f32[64,256]{1,0:T(8,128)S(1)}) custom-call(f32[16]{0:T(128)} %dif_in.1, f32[16,16]{1,0:T(8,128)} %rea_in.1, bf16[64,512]{1,0:T(8,128)(2,1)} %bitcast.12, f32[64,256]{1,0:T(8,128)} %bitcast.13, f32[16,256,128]{2,1,0:T(8,128)} %bitcast.9, f32[16,256,128]{2,1,0:T(8,128)} %bitcast.10, ...), custom_call_target="tpu_custom_call" | custom-call | tf_op jit(solution)/shard_map/section/pallas_call | solution.py:628
  64.1 1.4 %finish.1 = (f32[16,256,128]{2,1,0:T(8,128)}, f32[8,512]{1,0:T(8,128)}, f32[64,256]{1,0:T(8,128)}) custom-call(f32[16,256,128]{2,1,0:T(8,128)S(1)} %get-tuple-element.9.new, f32[8,512]{1,0:T(8,128)S(1)} %get-tuple-element.10.gram, f32[64,256]{1,0:T(8,128)S(1)} %get-tuple-element.11.product), custom_call_target="tpu_custom_call" | custom-call | tf_op jit(solution)/shard_map/finish/pallas_call | solution.py:688

commit v4 on v3

--- a/solution.py
+++ b/solution.py
@@ -43,9 +43,11 @@
     plane = gy * 4 + cy
     column = (zhi * 4 + cz) * 2 + core
     buffer_slab = ga == NA - 1
-    first_chip = zhi == 0
-    second_chip = zhi == 1
     diagonal = gy == ga
+    at_end = jnp.logical_or(cz == 0, cz == 3)
+    plain = jnp.logical_not(at_end)
+    first_chip = jnp.logical_and(at_end, zhi == 0)
+    second_chip = jnp.logical_and(at_end, zhi == 1)
     to_second = jnp.logical_and(first_chip, gy != ga + 2)
     from_first = jnp.logical_and(second_chip, diagonal)
     inner_slab = ga < NA - 1
@@ -242,7 +244,7 @@
         )
 
     def hand_over(c):
-        @pl.when(c < last)
+        @pl.when(jnp.logical_or(plain, c < last))
         def _():
             full[c, ga] = snap[c, ga]
             for j in (2, 3, 1):
@@ -430,6 +432,10 @@
 
     lax.fori_loop(0, last, gather_gram, 0)
 
+    @pl.when(plain)
+    def _():
+        gather_gram(jnp.int32(last), 0)
+
     @pl.when(first_chip)
     def _():
         def extra(block, carry):
@@ -553,6 +559,10 @@
         return carry
 
     lax.fori_loop(0, last, sent, 0)
+
+    @pl.when(plain)
+    def _():
+        sent(last, 0)
 
     @pl.when(first_chip)
     def _():

time: 65.6 us -> 64.9 us (0.989)
  no operation moved by 1% of the time
where the time goes in v4:
time: 64.9 us
  Pallas kernels  64.2 us (99%)
    pallas_call x1, Pallas kernels, shards(): pl.pallas_call(kernel, out_shape=(pltpu.VMEM((V, ROWS, XN), F32), pltpu.V...  62.9 us
    pallas_call x1, Pallas kernels, shards(): pl.pallas_call(finish, out_shape=(jax.ShapeDtypeStruct((V, ROWS, XN), F32...  1.35 us

profile of v4, /device:TPU:1, one launch (start us, length us, event | category | flops | bytes accessed | tf_op | source)
XLA Modules:
  0.0 64.9 jit_solution(7640555899377593182)
XLA Ops:
  0.6 62.9 %section.1 = (f32[16,256,128]{2,1,0:T(8,128)S(1)}, f32[8,512]{1,0:T(8,128)S(1)}, f32[64,256]{1,0:T(8,128)S(1)}) custom-call(f32[16]{0:T(128)} %dif_in.1, f32[16,16]{1,0:T(8,128)} %rea_in.1, bf16[64,512]{1,0:T(8,128)(2,1)} %bitcast.12, f32[64,256]{1,0:T(8,128)} %bitcast.13, f32[16,256,128]{2,1,0:T(8,128)} %bitcast.9, f32[16,256,128]{2,1,0:T(8,128)} %bitcast.10, ...), custom_call_target="tpu_custom_call" | custom-call | tf_op jit(solution)/shard_map/section/pallas_call | solution.py:638
  63.5 1.4 %finish.1 = (f32[16,256,128]{2,1,0:T(8,128)}, f32[8,512]{1,0:T(8,128)}, f32[64,256]{1,0:T(8,128)}) custom-call(f32[16,256,128]{2,1,0:T(8,128)S(1)} %get-tuple-element.9.new, f32[8,512]{1,0:T(8,128)S(1)} %get-tuple-element.10.gram, f32[64,256]{1,0:T(8,128)S(1)} %get-tuple-element.11.product), custom_call_target="tpu_custom_call" | custom-call | tf_op jit(solution)/shard_map/finish/pallas_call | solution.py:698

commit v5 on v4

--- a/solution.py
+++ b/solution.py
@@ -212,8 +212,8 @@
     def _():
         x_copy(1).start()
 
-    for c in range(1, NC):
-        start_faces(c)
+    start_faces(1)
+    start_faces(2)
 
     def exchange(c, j):
         peer = (ga + j) % NA
@@ -326,6 +326,10 @@
                 z_copy(0, c).wait_recv()
 
             faces_sent(c)
+
+            @pl.when(c < NC - 3)
+            def _():
+                start_faces(c + 3)
 
             for z in range(ZN):
                 first = PAD + c * CR + z

time: 64.9 us -> 64.7 us (level)
  no operation moved by 1% of the time
where the time goes in v5:
time: 64.7 us; the launch traced here: 64.6 us
  Pallas kernels  64 us (99%)
    pallas_call x1, Pallas kernels, shards(): pl.pallas_call(kernel, out_shape=(pltpu.VMEM((V, ROWS, XN), F32), pltpu.V...  62.6 us
    pallas_call x1, Pallas kernels, shards(): pl.pallas_call(finish, out_shape=(jax.ShapeDtypeStruct((V, ROWS, XN), F32...  1.35 us

profile of v5, /device:TPU:1, one launch (start us, length us, event | category | flops | bytes accessed | tf_op | source)
XLA Modules:
  0.0 64.6 jit_solution(11497820086101381710)
XLA Ops:
  0.6 62.6 %section.1 = (f32[16,256,128]{2,1,0:T(8,128)S(1)}, f32[8,512]{1,0:T(8,128)S(1)}, f32[64,256]{1,0:T(8,128)S(1)}) custom-call(f32[16]{0:T(128)} %dif_in.1, f32[16,16]{1,0:T(8,128)} %rea_in.1, bf16[64,512]{1,0:T(8,128)(2,1)} %bitcast.12, f32[64,256]{1,0:T(8,128)} %bitcast.13, f32[16,256,128]{2,1,0:T(8,128)} %bitcast.9, f32[16,256,128]{2,1,0:T(8,128)} %bitcast.10, ...), custom_call_target="tpu_custom_call" | custom-call | tf_op jit(solution)/shard_map/section/pallas_call | solution.py:642
  63.3 1.4 %finish.1 = (f32[16,256,128]{2,1,0:T(8,128)}, f32[8,512]{1,0:T(8,128)}, f32[64,256]{1,0:T(8,128)}) custom-call(f32[16,256,128]{2,1,0:T(8,128)S(1)} %get-tuple-element.9.new, f32[8,512]{1,0:T(8,128)S(1)} %get-tuple-element.10.gram, f32[64,256]{1,0:T(8,128)S(1)} %get-tuple-element.11.product), custom_call_target="tpu_custom_call" | custom-call | tf_op jit(solution)/shard_map/finish/pallas_call | solution.py:702

commit v6 on v5

--- a/solution.py
+++ b/solution.py
@@ -58,6 +58,35 @@
     def column_device(index):
         return (gy, cy * 4 + (index // 2) % 4, (index // 8) * 2 + index % 2)
 
+    barrier = pltpu.get_barrier_semaphore()
+    wrap_up = jnp.logical_and(cz == 3, gz < NZ - 1)
+    wrap_down = jnp.logical_and(cz == 0, gz > 0)
+
+    @pl.when(wrap_up)
+    def _():
+        pl.semaphore_signal(barrier, inc=1, device_id=(gy, gz + 1, ga), device_id_type=MESH)
+
+    @pl.when(wrap_down)
+    def _():
+        pl.semaphore_signal(barrier, inc=1, device_id=(gy, gz - 1, ga), device_id_type=MESH)
+
+    def greet(j, carry):
+        pl.semaphore_signal(barrier, inc=1, device_id=plane_device((plane + j) % 16), device_id_type=MESH)
+        pl.semaphore_signal(barrier, inc=1, device_id=column_device((column + j) % 16), device_id_type=MESH)
+        return carry
+
+    for j in (8, 9, 7, 10, 6, 11, 5, 12, 4, 13, 3, 14, 2, 15, 1):
+        greet(j, 0)
+
+    @pl.when(to_second)
+    def _():
+        pl.semaphore_signal(barrier, inc=1, device_id=(ga + 2, gz, ga + 2), device_id_type=MESH)
+
+    @pl.when(from_first)
+    def _():
+        for j in range(1, NY):
+            pl.semaphore_signal(barrier, inc=1, device_id=((gy + j) % NY, gz, ga - 2), device_id_type=MESH)
+
     load_f = pltpu.make_async_copy(fields, fbuf.at[:, pl.ds(PAD, ROWS), :], load_sem.at[0])
     load_s = pltpu.make_async_copy(start, sbuf, load_sem.at[1])
     load_v = pltpu.make_async_copy(vel, vbuf, load_sem.at[2])
@@ -71,35 +100,6 @@
     load_v.start()
     for copy in load_small[1:]:
         copy.start()
-
-    barrier = pltpu.get_barrier_semaphore()
-    wrap_up = jnp.logical_and(cz == 3, gz < NZ - 1)
-    wrap_down = jnp.logical_and(cz == 0, gz > 0)
-
-    @pl.when(wrap_up)
-    def _():
-        pl.semaphore_signal(barrier, inc=1, device_id=(gy, gz + 1, ga), device_id_type=MESH)
-
-    @pl.when(wrap_down)
-    def _():
-        pl.semaphore_signal(barrier, inc=1, device_id=(gy, gz - 1, ga), device_id_type=MESH)
-
-    def greet(j, carry):
-        pl.semaphore_signal(barrier, inc=1, device_id=plane_device((plane + j) % 16), device_id_type=MESH)
-        pl.semaphore_signal(barrier, inc=1, device_id=column_device((column + j) % 16), device_id_type=MESH)
-        return carry
-
-    for j in range(1, 16):
-        greet(j, 0)
-
-    @pl.when(to_second)
-    def _():
-        pl.semaphore_signal(barrier, inc=1, device_id=(ga + 2, gz, ga + 2), device_id_type=MESH)
-
-    @pl.when(from_first)
-    def _():
-        for j in range(1, NY):
-            pl.semaphore_signal(barrier, inc=1, device_id=((gy + j) % NY, gz, ga - 2), device_id_type=MESH)
 
     @pl.when(gy == 0)
     def _():

time: 64.7 us -> 64.5 us (level)
  no operation moved by 1% of the time
where the time goes in v6:
time: 64.5 us
  Pallas kernels  63.8 us (99%)
    pallas_call x1, Pallas kernels, shards(): pl.pallas_call(kernel, out_shape=(pltpu.VMEM((V, ROWS, XN), F32), pltpu.V...  62.5 us
    pallas_call x1, Pallas kernels, shards(): pl.pallas_call(finish, out_shape=(jax.ShapeDtypeStruct((V, ROWS, XN), F32...  1.35 us

profile of v6, /device:TPU:1, one launch (start us, length us, event | category | flops | bytes accessed | tf_op | source)
XLA Modules:
  0.0 64.5 jit_solution(12529306793549968192)
XLA Ops:
  0.6 62.5 %section.1 = (f32[16,256,128]{2,1,0:T(8,128)S(1)}, f32[8,512]{1,0:T(8,128)S(1)}, f32[64,256]{1,0:T(8,128)S(1)}) custom-call(f32[16]{0:T(128)} %dif_in.1, f32[16,16]{1,0:T(8,128)} %rea_in.1, bf16[64,512]{1,0:T(8,128)(2,1)} %bitcast.12, f32[64,256]{1,0:T(8,128)} %bitcast.13, f32[16,256,128]{2,1,0:T(8,128)} %bitcast.9, f32[16,256,128]{2,1,0:T(8,128)} %bitcast.10, ...), custom_call_target="tpu_custom_call" | custom-call | tf_op jit(solution)/shard_map/section/pallas_call | solution.py:642
  63.1 1.4 %finish.1 = (f32[16,256,128]{2,1,0:T(8,128)}, f32[8,512]{1,0:T(8,128)}, f32[64,256]{1,0:T(8,128)}) custom-call(f32[16,256,128]{2,1,0:T(8,128)S(1)} %get-tuple-element.9.new, f32[8,512]{1,0:T(8,128)S(1)} %get-tuple-element.10.gram, f32[64,256]{1,0:T(8,128)S(1)} %get-tuple-element.11.product), custom_call_target="tpu_custom_call" | custom-call | tf_op jit(solution)/shard_map/finish/pallas_call | solution.py:702
